TPU v7x, 128 devices: a whole 4x4x4 slice. The times are simulated.
128 devices in a mesh: ctx: 32 (over y, x, core), fsdp: 4 (over z).
Axes of the slice: x: 4, y: 4, z: 4, core: 2. Of those that a mesh axis runs over, the one named last changes fastest.
Arguments:
- activations: bfloat16 [8, 4096, 960], P('fsdp', 'ctx'), may hold values from -6 to 6
- cotangent: bfloat16 [8, 4096, 960], P('fsdp', 'ctx'), may hold values from -6 to 6
- block_order: int32 [64], replicated, may hold values from 0 to 63, as said below
- attend_gain: bfloat16 [960], P('fsdp'), may hold values from 0.099609375 to 1.8984375
- query_weight: bfloat16 [960, 960], P('fsdp'), may hold values from -0.1875 to 0.1875
- key_weight: bfloat16 [960, 320], P('fsdp'), may hold values from -0.1875 to 0.1875
- value_weight: bfloat16 [960, 320], P('fsdp'), may hold values from -0.1875 to 0.1875
- output_weight: bfloat16 [960, 960], P('fsdp'), may hold values from -2 to 2
- dense_gain: bfloat16 [960], P('fsdp'), may hold values from 0.099609375 to 1.8984375
- gate_weight: bfloat16 [960, 2560], P('fsdp'), may hold values from -0.1875 to 0.1875
- up_weight: bfloat16 [960, 2560], P('fsdp'), may hold values from -0.1875 to 0.1875
- down_weight: bfloat16 [2560, 960], P('fsdp'), may hold values from -0.125 to 0.125
Outputs:
- layer_output: bfloat16 [8, 4096, 960], P('fsdp', 'ctx')
- input_grads: float32 [8, 4096, 960], P('fsdp', 'ctx')
- attend_gain_grads: float32 [960], P('fsdp')
- query_grads: float32 [960, 960], P('fsdp')
- key_grads: float32 [960, 320], P('fsdp')
- value_grads: float32 [960, 320], P('fsdp')
- output_grads: float32 [960, 960], P('fsdp')
- dense_gain_grads: float32 [960], P('fsdp')
- gate_grads: float32 [960, 2560], P('fsdp')
- up_grads: float32 [960, 2560], P('fsdp')
- down_grads: float32 [2560, 960], P('fsdp')
Inputs may be any that keep to these rules, and one draw needn't show every extreme that they name: block_order is a permutation of 0 to 63 in which the entries 2 c and 2 c + 1 add up to 63 for every c.
All inputs are finite; a program needn't handle non-finite values.
Results may differ from a plain program's by a relative error of at most 0.03.
Values may be sent and summed in bfloat16 or wider, within the bound.
No kernel may reach another device: no remote copies, remote signals or barrier semaphores. Data moves between devices by JAX's collectives and lax.ppermute only.
A program may use at most 192 MiB of HBM per device.

v0:
```python
import jax
import jax.numpy as jnp
from jax import lax
from jax.sharding import PartitionSpec as P

HEADS = 15
KV_HEADS = 5
HEAD = 64
BLOCK = 512


EPSILON = 1e-05
THETA = 100000.0
SCALE = 0.125
MASKED = -1e30


def product(form, left, right):
    return jnp.einsum(form, left, right, preferred_element_type=jnp.float32)


def rope_tables(places, head_size):
    pair_ids = jnp.arange(head_size // 2, dtype=jnp.float32)
    frequency = THETA ** (-2.0 * pair_ids / head_size)
    angles = places.astype(jnp.float32)[:, None] * frequency[None, :]
    angles = jnp.concatenate([angles, angles], axis=1)
    return (jnp.cos(angles), jnp.sin(angles))


def turn_half(heads, head_size):
    return jnp.concatenate([-heads[..., head_size // 2 :], heads[..., : head_size // 2]], axis=-1)


def rotate(values, cosine, sine_table, head_size):
    row_count = values.shape[0]
    heads = values.reshape(row_count, -1, head_size)
    turned = heads * cosine[:, None, :] + turn_half(heads, head_size) * sine_table[:, None, :]
    return turned.reshape(row_count, -1)


def rotate_back(grad_rows, cosine, sine_table, head_size):
    row_count = grad_rows.shape[0]
    heads = grad_rows.reshape(row_count, -1, head_size)
    turned = heads * cosine[:, None, :] - turn_half(heads * sine_table[:, None, :], head_size)
    return turned.reshape(row_count, -1)


def norm_back(grad_normed, values, scale, gain):
    unit_rows = values * scale
    gain_grad = jnp.sum(grad_normed * unit_rows, axis=0)
    weighted = grad_normed * gain
    width = values.shape[-1]
    back_rows = scale * (
        weighted - unit_rows * (jnp.sum(weighted * unit_rows, axis=-1, keepdims=True) / width)
    )
    return (gain_grad, back_rows)


def key_block(sources, first_row, block_rows, kv_heads, head_size):
    return lax.dynamic_slice_in_dim(sources, first_row, block_rows, 0).reshape(
        block_rows, kv_heads, head_size
    )


def masked_scores(query_heads, keys_here, key_places, places):
    raw_scores = product("kgqd,skd->kgqs", query_heads, keys_here) * SCALE
    allowed = key_places[None, :] <= places[:, None]
    return jnp.where(allowed[None, None], raw_scores, MASKED)


def local(
    activations,
    cotangent,
    block_order,
    attend_gain,
    query_weight,
    key_weight,
    value_weight,
    output_weight,
    dense_gain,
    gate_weight,
    up_weight,
    down_weight,
):
    local_seqs = activations.shape[0]
    tokens = activations.shape[1]
    width = activations.shape[2]
    rows_all = local_seqs * tokens
    half_rows = tokens // 2
    length = tokens * lax.axis_size("ctx")
    head_size = HEAD
    kv_heads = KV_HEADS
    group_size = HEADS // KV_HEADS
    kv_width = kv_heads * head_size
    block_rows = BLOCK
    block_count = length // block_rows
    row_ids = jnp.arange(length, dtype=jnp.int32)
    slot_ids = jnp.arange(block_order.shape[0], dtype=jnp.int32)
    matches = (row_ids // half_rows)[:, None] == slot_ids[None, :]
    places_all = (
        jnp.sum(jnp.where(matches, block_order[None, :], 0), axis=1) * half_rows
        + row_ids % half_rows
    )
    places = lax.dynamic_slice_in_dim(places_all, lax.axis_index("ctx") * tokens, tokens, 0)
    cosine_one, sine_one = rope_tables(places, head_size)
    cosine = jnp.tile(cosine_one, (local_seqs, 1))
    sine_table = jnp.tile(sine_one, (local_seqs, 1))
    inputs = activations.astype(jnp.float32).reshape(rows_all, width)
    blocks = jnp.arange(block_count, dtype=jnp.int32)
    attend_set = (
        lax.all_gather(attend_gain, "fsdp", axis=0, tiled=True),
        lax.all_gather(query_weight, "fsdp", axis=0, tiled=True),
        lax.all_gather(key_weight, "fsdp", axis=0, tiled=True),
        lax.all_gather(value_weight, "fsdp", axis=0, tiled=True),
        lax.all_gather(output_weight, "fsdp", axis=0, tiled=True),
    )
    gain_one = attend_set[0].astype(jnp.float32)
    scale_one = lax.rsqrt(jnp.mean(inputs * inputs, axis=-1, keepdims=True) + EPSILON)
    normed_one = (inputs * scale_one * gain_one).astype(jnp.bfloat16)
    queries = rotate(
        jnp.dot(normed_one, attend_set[1], preferred_element_type=jnp.float32),
        cosine,
        sine_table,
        head_size,
    ).astype(jnp.bfloat16)
    key_rows = rotate(
        jnp.dot(normed_one, attend_set[2], preferred_element_type=jnp.float32),
        cosine,
        sine_table,
        head_size,
    ).astype(jnp.bfloat16)
    values = jnp.dot(normed_one, attend_set[3], preferred_element_type=jnp.float32).astype(
        jnp.bfloat16
    )
    key_local = key_rows.reshape(local_seqs, tokens, kv_width)
    value_local = values.reshape(local_seqs, tokens, kv_width)
    all_keys, all_values = (
        lax.all_gather(key_local, "ctx", axis=1, tiled=True),
        lax.all_gather(value_local, "ctx", axis=1, tiled=True),
    )
    query_seq = queries.reshape(local_seqs, tokens, kv_heads, group_size, head_size).transpose(
        0, 2, 3, 1, 4
    )
    start_top = jnp.full((kv_heads, group_size, tokens), MASKED, jnp.float32)
    log_totals = []
    attended_list = []
    for seq_index in range(local_seqs):
        query_heads = query_seq[seq_index]
        seq_keys = all_keys[seq_index]
        seq_values = all_values[seq_index]

        def stats_step(state_pair, block_index):
            running_top, running_sum = state_pair
            first_row = block_index * block_rows
            keys_here = key_block(seq_keys, first_row, block_rows, kv_heads, head_size)
            scores = masked_scores(
                query_heads,
                keys_here,
                lax.dynamic_slice_in_dim(places_all, first_row, block_rows, 0),
                places,
            )
            new_top = jnp.maximum(running_top, jnp.max(scores, axis=-1))
            running_sum = running_sum * jnp.exp(running_top - new_top) + jnp.sum(
                jnp.exp(scores - new_top[..., None]), axis=-1
            )
            return ((new_top, running_sum), None)

        (final_top, final_sum), unused = lax.scan(
            stats_step, (start_top, jnp.zeros_like(start_top)), blocks
        )
        log_total = final_top + jnp.log(final_sum)

        def output_step(accumulated, block_index):
            first_row = block_index * block_rows
            keys_here = key_block(seq_keys, first_row, block_rows, kv_heads, head_size)
            values_here = key_block(seq_values, first_row, block_rows, kv_heads, head_size)
            scores = masked_scores(
                query_heads,
                keys_here,
                lax.dynamic_slice_in_dim(places_all, first_row, block_rows, 0),
                places,
            )
            weights_soft = jnp.exp(scores - log_total[..., None]).astype(jnp.bfloat16)
            return (accumulated + product("kgqs,skd->kgqd", weights_soft, values_here), None)

        attended_heads, unused = lax.scan(
            output_step, jnp.zeros((kv_heads, group_size, tokens, head_size), jnp.float32), blocks
        )
        log_totals.append(log_total)
        attended_list.append(attended_heads)
    attended_seq = jnp.stack(attended_list, axis=0)
    attended = attended_seq.transpose(0, 3, 1, 2, 4).reshape(rows_all, -1).astype(jnp.bfloat16)
    middle = inputs + jnp.dot(attended, attend_set[4], preferred_element_type=jnp.float32)
    dense_set = (
        lax.all_gather(dense_gain, "fsdp", axis=0, tiled=True),
        lax.all_gather(gate_weight, "fsdp", axis=0, tiled=True),
        lax.all_gather(up_weight, "fsdp", axis=0, tiled=True),
        lax.all_gather(down_weight, "fsdp", axis=0, tiled=True),
    )
    gain_two = dense_set[0].astype(jnp.float32)
    scale_two = lax.rsqrt(jnp.mean(middle * middle, axis=-1, keepdims=True) + EPSILON)
    normed_two = (middle * scale_two * gain_two).astype(jnp.bfloat16)
    gate_rows = jnp.dot(normed_two, dense_set[1], preferred_element_type=jnp.float32)
    upper = jnp.dot(normed_two, dense_set[2], preferred_element_type=jnp.float32)
    sigmoid_gate = jax.nn.sigmoid(gate_rows)
    hidden = (gate_rows * sigmoid_gate * upper).astype(jnp.bfloat16)
    layer_output = (
        middle + jnp.dot(hidden, dense_set[3], preferred_element_type=jnp.float32)
    ).astype(jnp.bfloat16)
    back_dense = (
        lax.all_gather(dense_gain, "fsdp", axis=0, tiled=True),
        lax.all_gather(gate_weight, "fsdp", axis=0, tiled=True),
        lax.all_gather(up_weight, "fsdp", axis=0, tiled=True),
        lax.all_gather(down_weight, "fsdp", axis=0, tiled=True),
    )
    back_attend = (
        lax.all_gather(attend_gain, "fsdp", axis=0, tiled=True),
        lax.all_gather(query_weight, "fsdp", axis=0, tiled=True),
        lax.all_gather(key_weight, "fsdp", axis=0, tiled=True),
        lax.all_gather(value_weight, "fsdp", axis=0, tiled=True),
        lax.all_gather(output_weight, "fsdp", axis=0, tiled=True),
    )
    back_keys, back_values = (
        lax.all_gather(key_local, "ctx", axis=1, tiled=True),
        lax.all_gather(value_local, "ctx", axis=1, tiled=True),
    )
    grad_low = cotangent.reshape(rows_all, width)
    grad_out = grad_low.astype(jnp.float32)
    down_grad = product("tf,td->fd", hidden, grad_low)
    grad_hidden = product("td,fd->tf", grad_low, back_dense[3])
    grad_gate = (
        grad_hidden * upper * sigmoid_gate * (1.0 + gate_rows * (1.0 - sigmoid_gate))
    ).astype(jnp.bfloat16)
    grad_upper = (grad_hidden * gate_rows * sigmoid_gate).astype(jnp.bfloat16)
    gate_grad = product("td,tf->df", normed_two, grad_gate)
    up_grad = product("td,tf->df", normed_two, grad_upper)
    grad_normed_two = product("tf,df->td", grad_gate, back_dense[1]) + product(
        "tf,df->td", grad_upper, back_dense[2]
    )
    dense_gain_grad, norm_two_back = norm_back(grad_normed_two, middle, scale_two, gain_two)
    grad_middle = grad_out + norm_two_back
    grad_branch = grad_middle.astype(jnp.bfloat16)
    output_grad = product("te,td->ed", attended, grad_branch)
    grad_attended = product("td,ed->te", grad_branch, back_attend[4]).astype(jnp.bfloat16)
    grad_seq = grad_attended.reshape(local_seqs, tokens, kv_heads, group_size, head_size).transpose(
        0, 2, 3, 1, 4
    )
    query_list = []
    key_list = []
    value_list = []
    for seq_index in range(local_seqs):
        query_heads = query_seq[seq_index]
        grad_heads = grad_seq[seq_index]
        log_total = log_totals[seq_index]
        seq_keys = back_keys[seq_index]
        seq_values = back_values[seq_index]
        softmax_dot = jnp.sum(grad_heads.astype(jnp.float32) * attended_list[seq_index], axis=-1)

        def back_step(grad_query, block_index):
            first_row = block_index * block_rows
            keys_here = key_block(seq_keys, first_row, block_rows, kv_heads, head_size)
            values_here = key_block(seq_values, first_row, block_rows, kv_heads, head_size)
            scores = masked_scores(
                query_heads,
                keys_here,
                lax.dynamic_slice_in_dim(places_all, first_row, block_rows, 0),
                places,
            )
            weights_soft = jnp.exp(scores - log_total[..., None])
            grad_weights = product("kgqd,skd->kgqs", grad_heads, values_here)
            grad_scores = (weights_soft * (grad_weights - softmax_dot[..., None])).astype(
                jnp.bfloat16
            )
            grad_query = grad_query + product("kgqs,skd->kgqd", grad_scores, keys_here) * SCALE
            key_part = product("kgqs,kgqd->skd", grad_scores, query_heads) * SCALE
            value_part = product("kgqs,kgqd->skd", weights_soft.astype(jnp.bfloat16), grad_heads)
            return (grad_query, (key_part, value_part))

        grad_query, (key_parts, value_parts) = lax.scan(
            back_step, jnp.zeros((kv_heads, group_size, tokens, head_size), jnp.float32), blocks
        )
        query_list.append(grad_query)
        key_list.append(key_parts.reshape(length, kv_width))
        value_list.append(value_parts.reshape(length, kv_width))
    key_sum, value_sum = (
        lax.psum_scatter(
            jnp.stack(key_list, axis=0).astype(jnp.bfloat16), "ctx", scatter_dimension=1, tiled=True
        ).astype(jnp.float32),
        lax.psum_scatter(
            jnp.stack(value_list, axis=0).astype(jnp.bfloat16),
            "ctx",
            scatter_dimension=1,
            tiled=True,
        ).astype(jnp.float32),
    )
    grad_query_all = jnp.stack(query_list, axis=0).transpose(0, 3, 1, 2, 4).reshape(rows_all, -1)
    query_low = rotate_back(grad_query_all, cosine, sine_table, head_size).astype(jnp.bfloat16)
    key_low = rotate_back(
        key_sum.reshape(rows_all, kv_width), cosine, sine_table, head_size
    ).astype(jnp.bfloat16)
    value_low = value_sum.reshape(rows_all, kv_width).astype(jnp.bfloat16)
    query_grad = product("td,te->de", normed_one, query_low)
    key_grad = product("td,te->de", normed_one, key_low)
    value_grad = product("td,te->de", normed_one, value_low)
    grad_normed_one = (
        product("te,de->td", query_low, back_attend[1])
        + product("te,de->td", key_low, back_attend[2])
        + product("te,de->td", value_low, back_attend[3])
    )
    attend_gain_grad, norm_one_back = norm_back(grad_normed_one, inputs, scale_one, gain_one)
    input_grads = grad_middle + norm_one_back
    dense_shares = (
        lax.psum_scatter(
            dense_gain_grad.astype(jnp.bfloat16), "fsdp", scatter_dimension=0, tiled=True
        ).astype(jnp.float32),
        lax.psum_scatter(
            gate_grad.astype(jnp.bfloat16), "fsdp", scatter_dimension=0, tiled=True
        ).astype(jnp.float32),
        lax.psum_scatter(
            up_grad.astype(jnp.bfloat16), "fsdp", scatter_dimension=0, tiled=True
        ).astype(jnp.float32),
        lax.psum_scatter(
            down_grad.astype(jnp.bfloat16), "fsdp", scatter_dimension=0, tiled=True
        ).astype(jnp.float32),
    )
    attend_shares = (
        lax.psum_scatter(
            attend_gain_grad.astype(jnp.bfloat16), "fsdp", scatter_dimension=0, tiled=True
        ).astype(jnp.float32),
        lax.psum_scatter(
            query_grad.astype(jnp.bfloat16), "fsdp", scatter_dimension=0, tiled=True
        ).astype(jnp.float32),
        lax.psum_scatter(
            key_grad.astype(jnp.bfloat16), "fsdp", scatter_dimension=0, tiled=True
        ).astype(jnp.float32),
        lax.psum_scatter(
            value_grad.astype(jnp.bfloat16), "fsdp", scatter_dimension=0, tiled=True
        ).astype(jnp.float32),
        lax.psum_scatter(
            output_grad.astype(jnp.bfloat16), "fsdp", scatter_dimension=0, tiled=True
        ).astype(jnp.float32),
    )
    summed = (
        lax.psum(attend_shares[0].astype(jnp.bfloat16), "ctx").astype(jnp.float32),
        lax.psum(attend_shares[1].astype(jnp.bfloat16), "ctx").astype(jnp.float32),
        lax.psum(attend_shares[2].astype(jnp.bfloat16), "ctx").astype(jnp.float32),
        lax.psum(attend_shares[3].astype(jnp.bfloat16), "ctx").astype(jnp.float32),
        lax.psum(attend_shares[4].astype(jnp.bfloat16), "ctx").astype(jnp.float32),
        lax.psum(dense_shares[0].astype(jnp.bfloat16), "ctx").astype(jnp.float32),
        lax.psum(dense_shares[1].astype(jnp.bfloat16), "ctx").astype(jnp.float32),
        lax.psum(dense_shares[2].astype(jnp.bfloat16), "ctx").astype(jnp.float32),
        lax.psum(dense_shares[3].astype(jnp.bfloat16), "ctx").astype(jnp.float32),
    )
    return (
        layer_output.reshape(local_seqs, tokens, width),
        input_grads.reshape(local_seqs, tokens, width),
        summed[0],
        summed[1],
        summed[2],
        summed[3],
        summed[4],
        summed[5],
        summed[6],
        summed[7],
        summed[8],
    )


def solution(mesh):
    in_specs = (
        P("fsdp", "ctx", None),
        P("fsdp", "ctx", None),
        P(),
        P("fsdp"),
        P("fsdp", None),
        P("fsdp", None),
        P("fsdp", None),
        P("fsdp", None),
        P("fsdp"),
        P("fsdp", None),
        P("fsdp", None),
        P("fsdp", None),
    )
    out_specs = (
        P("fsdp", "ctx", None),
        P("fsdp", "ctx", None),
        P("fsdp"),
        P("fsdp", None),
        P("fsdp", None),
        P("fsdp", None),
        P("fsdp", None),
        P("fsdp"),
        P("fsdp", None),
        P("fsdp", None),
        P("fsdp", None),
    )
    return jax.shard_map(local, mesh=mesh, in_specs=in_specs, out_specs=out_specs, check_vma=False)
```

profile of v0, /device:TPU:1, one launch (start us, length us, event | category | flops | bytes accessed | tf_op | source)
XLA Modules:
  0.0 1182.5 jit_solution(1431357684981016128)
XLA Ops:
  13.0 10.6 all-reduce.7
  27.7 14.8 %all-gather = bf16[4,240,320]{1,2,0:T(8,128)(2,1)S(1)} all-gather(bf16[1,240,320]{1,2,0:T(8,128)(2,1)S(1)} %bitcast.622), channel_id=1, replica_groups=mesh['ctx'=32,'fsdp'=4] {'fsdp'}, dimensions={0}, use_global_device_ids=true | all-gather | bytes 768000 | tf_op jit(solution)/shard_map/all_gather | solution.py:113
  45.4 10.7 all-gather.1
  69.8 33.1 %all-gather.10.cloned.1.call-done = bf16[2,4096,320]{1,2,0:T(8,128)(2,1)} async-done(((bf16[2,128,320]{1,2,0:T(8,128)(2,1)}), bf16[2,4096,320]{1,2,0:T(8,128)(2,1)}) %all-gather.10.cloned.1.call-update) | async-done | bytes 5242896 | tf_op jit(solution)/shard_map/all_gather | solution.py:138
  108.4 65.4 %while.78 = (s32[]{:T(128)}, f32[5,3,128]{2,1,0:T(4,128)S(1)}, f32[5,3,128]{2,1,0:T(4,128)S(1)}, s32[8]{0:T(128)S(1)}, s32[4096]{0:T(1024)S(1)}, /*index=5*/s32[...) while((s32[]{:T(128)}, f32[5,3,128]{2,1,0:T(4,128)S(1)}, ...), condition=%wide.region_5.6_spmd.clone, body=%wide.region_2.5_spmd.clone.sunk | while | flops 132785544 | bytes 9396418 | solution.py:168
  179.5 32.4 %while.79 = (s32[]{:T(128)}, f32[5,3,128,64]{2,3,1,0:T(8,128)S(1)}, s32[8]{0:T(128)S(1)}, s32[4096]{0:T(1024)S(1)}, s32[128]{0:T(128)S(1)}, /*index=5*/bf16[4096...) while((s32[]{:T(128)}, f32[5,3,128,64]{2,3,1,0:T(8,128)S(1)}, ...), condition=%wide.region_7.8_spmd.clone, body=%wide.region_6.7_spmd.clone.sunk | while | flops 255901696 | bytes 3340489 | solution.py:186
  212.5 65.2 %while.80 = (s32[]{:T(128)}, f32[5,3,128]{2,1,0:T(4,128)S(1)}, f32[5,3,128]{2,1,0:T(4,128)S(1)}, s32[8]{0:T(128)S(1)}, s32[4096]{0:T(1024)S(1)}, /*index=5*/s32[...) while((s32[]{:T(128)}, f32[5,3,128]{2,1,0:T(4,128)S(1)}, ...), condition=%wide.region_11.12_spmd.clone, body=%wide.region_8.11_spmd.clone.sunk | while | flops 132785544 | bytes 9396418 | solution.py:168
  277.7 32.6 %while.81 = (s32[]{:T(128)}, f32[5,3,128,64]{2,3,1,0:T(8,128)S(1)}, s32[8]{0:T(128)S(1)}, s32[4096]{0:T(1024)S(1)}, s32[128]{0:T(128)S(1)}, /*index=5*/bf16[4096...) while((s32[]{:T(128)}, f32[5,3,128,64]{2,3,1,0:T(8,128)S(1)}, ...), condition=%wide.region_13.14_spmd.clone, body=%wide.region_12.13_spmd.clone.sunk | while | flops 255901696 | bytes 3340489 | solution.py:186
  325.9 30.4 %all-gather.22.cloned.1.call-done = bf16[2560,960]{0,1:T(8,128)(2,1)} async-done(((bf16[640,960]{0,1:T(8,128)(2,1)}), bf16[2560,960]{0,1:T(8,128)(2,1)}) %all-gather.22.cloned.1.call-update) | async-done | bytes 4915216 | tf_op jit(solution)/shard_map/all_gather | solution.py:198
  378.7 87.0 %while.82 = (s32[]{:T(128)}, f32[5,3,128,64]{2,3,1,0:T(8,128)}, bf16[8,512,5,64]{1,3,2,0:T(8,128)(2,1)}, bf16[8,512,5,64]{1,3,2,0:T(8,128)(2,1)}, s32[8]{0:T(128...) while((s32[]{:T(128)}, f32[5,3,128,64]{2,3,1,0:T(8,128)}, ...), condition=%wide.region_18.19_spmd.clone, body=%wide.region_17.18_spmd.clone.sunk | while | flops 639574016 | bytes 23554336 | solution.py:279
  476.3 73.7 %while.83 = (s32[]{:T(128)}, f32[5,3,128,64]{2,3,1,0:T(8,128)S(1)}, bf16[8,512,5,64]{1,3,2,0:T(8,128)(2,1)}, bf16[8,512,5,64]{1,3,2,0:T(8,128)(2,1)}, s32[8]{0:T...) while((s32[]{:T(128)}, f32[5,3,128,64]{2,3,1,0:T(8,128)S(1)}, ...), condition=%wide.region_21.22_spmd.clone, body=%wide.region_20.21_spmd.clone.sunk | while | flops 639574016 | bytes 24506656 | solution.py:279
  565.5 16.1 %copy.186 = bf16[2,4096,320]{2,0,1:T(2,128)(2,1)} copy(bf16[2,4096,320]{1,2,0:T(8,128)(2,1)} %pad_maximum_fusion.1) | data formatting | bytes 10485760
  581.6 13.1 %reshape.528 = bf16[4096,640]{1,0:T(8,128)(2,1)} reshape(bf16[4096,2,320]{2,1,0:T(2,128)(2,1)} %bitcast.583) | data formatting | bytes 10485760
  620.4 16.2 %copy.184 = bf16[2,4096,320]{2,0,1:T(2,128)(2,1)} copy(bf16[2,4096,320]{1,2,0:T(8,128)(2,1)} %pad_maximum_fusion) | data formatting | bytes 10485760
  636.6 13.1 %reshape.526 = bf16[4096,640]{1,0:T(8,128)(2,1)} reshape(bf16[4096,2,320]{2,1,0:T(2,128)(2,1)} %bitcast.584) | data formatting | bytes 10485760
  649.8 28.3 %reduce-scatter.30.cloned.1.call-done = bf16[128,640]{1,0:T(8,128)(2,1)} async-done(((bf16[4096,640]{1,0:T(8,128)(2,1)}), bf16[128,640]{1,0:T(8,128)(2,1)}) %reduce-scatter.30.cloned.1.call-update) | async-done | bytes 163856
  680.9 85.3 %reduce-scatter.28.cloned.1.call-done = bf16[128,640]{1,0:T(8,128)(2,1)} async-done(((bf16[4096,640]{1,0:T(8,128)(2,1)}), bf16[128,640]{1,0:T(8,128)(2,1)}) %reduce-scatter.28.cloned.1.call-update) | async-done | bytes 163856
  817.2 56.9 %reduce-scatter.36.cloned.1.call-done = bf16[640,960]{1,0:T(8,128)(2,1)} async-done(((bf16[2560,960]{1,0:T(8,128)(2,1)}), bf16[640,960]{1,0:T(8,128)(2,1)}) %reduce-scatter.36.cloned.1.call-update) | async-done | bytes 1228816
  876.5 29.0 %reduce-scatter.20.cloned.1.call-done = bf16[240,960]{1,0:T(8,128)(2,1)} async-done(((bf16[960,960]{1,0:T(8,128)(2,1)}), bf16[240,960]{1,0:T(8,128)(2,1)}) %reduce-scatter.20.cloned.1.call-update) | async-done | bytes 460816 | tf_op jit(solution)/shard_map/reduce_scatter | solution.py:330
  905.5 31.3 %reduce-scatter.22.cloned.1.call-done = bf16[240,960]{1,0:T(8,128)(2,1)} async-done(((bf16[960,960]{1,0:T(8,128)(2,1)}), bf16[240,960]{1,0:T(8,128)(2,1)}) %reduce-scatter.22.cloned.1.call-update) | async-done | bytes 460816 | tf_op jit(solution)/shard_map/reduce_scatter | solution.py:339
  936.8 54.8 %reduce-scatter.24.cloned.1.call-done = bf16[240,2560]{1,0:T(8,128)(2,1)} async-done(((bf16[960,2560]{1,0:T(8,128)(2,1)}), bf16[240,2560]{1,0:T(8,128)(2,1)}) %reduce-scatter.24.cloned.1.call-update) | async-done | bytes 1228816 | tf_op jit(solution)/shard_map/reduce_scatter | solution.py:316
  991.6 55.0 %reduce-scatter.26.cloned.1.call-done = bf16[240,2560]{1,0:T(8,128)(2,1)} async-done(((bf16[960,2560]{1,0:T(8,128)(2,1)}), bf16[240,2560]{1,0:T(8,128)(2,1)}) %reduce-scatter.26.cloned.1.call-update) | async-done | bytes 1228816 | tf_op jit(solution)/shard_map/reduce_scatter | solution.py:319
  1065.3 64.8 %all-reduce.4 = (bf16[240]{0:T(256)(128)(2,1)S(1)}, bf16[240]{0:T(256)(128)(2,1)S(1)}) all-reduce(bf16[240]{0:T(256)(128)(2,1)S(1)} %dynamic-slice.3, bf16[240]{0:T(256)(128)(2,1)S(1)} %dynamic-slice.5), channel_id=1, replica_groups=mesh['ctx'=32,'fsdp'=4] {'ctx'}, use_global_device_ids=true, to_apply=%region_27.28 | all-reduce | flops 480 | bytes 1920 | tf_op jit(solution)/shard_map/psum | solution.py:344
  1132.5 33.2 %all-reduce.10.cloned.1.call-done = (bf16[240,960]{1,0:T(8,128)(2,1)}, bf16[240,320]{0,1:T(8,128)(2,1)}, bf16[240,320]{0,1:T(8,128)(2,1)}, bf16[240,960]{1,0:T(8...) async-done(((bf16[240,960]{1,0:T(8,128)(2,1)}, bf16[240,320]{0,1:T(8,128)(2,1)}, bf16[240,320]{0,1:T(8,128)(2,1)}, ...) | async-done | bytes 4915216 | tf_op jit(solution)/shard_map/psum | solution.py:345
  (725 shorter events, 534.9 us)
Async XLA Ops:
  7.2 349.1 %copy-start = (bf16[2,128,960]{1,2,0:T(8,128)(2,1)S(1)}, bf16[2,128,960]{1,2,0:T(8,128)(2,1)}, u32[]{:S(2)}) copy-start(bf16[2,128,960]{1,2,0:T(8,128)(2,1)} %param.25) | copy-start | bytes 1474564
  7.2 54.1 %all-gather.12.cloned.1.call-start = ((), (), s32[]{:S(2)}) async-start(), calls=%async_computation.10 | async-start | bytes 2457600 | tf_op jit(solution)/shard_map/all_gather | solution.py:112
  7.9 94.9 %all-gather.10.cloned.1.call-start = ((), (), s32[]{:S(2)}) async-start(), calls=%async_computation.9 | async-start | bytes 5406720 | tf_op jit(solution)/shard_map/all_gather | solution.py:138
  45.4 128.5 %all-gather.14.cloned.1.call-start = ((), (), s32[]{:S(2)}) async-start(), calls=%async_computation.11 | async-start | bytes 5406720 | tf_op jit(solution)/shard_map/all_gather | solution.py:139
  58.4 253.1 %all-gather.16.cloned.1.call-start = ((), (), s32[]{:S(2)}) async-start(), calls=%async_computation.12 | async-start | bytes 2457600 | tf_op jit(solution)/shard_map/all_gather | solution.py:115
  59.0 255.6 %all-gather.18.cloned.1.call-start = ((), (), s32[]{:S(2)}) async-start(), calls=%async_computation.13 | async-start | bytes 6144000 | tf_op jit(solution)/shard_map/all_gather | solution.py:196
  59.6 260.8 %all-gather.20.cloned.1.call-start = ((), (), s32[]{:S(2)}) async-start(), calls=%async_computation.14 | async-start | bytes 6144000 | tf_op jit(solution)/shard_map/all_gather | solution.py:197
  60.2 296.1 %all-gather.22.cloned.1.call-start = ((), (), s32[]{:S(2)}) async-start(), calls=%async_computation.15 | async-start | bytes 6144000 | tf_op jit(solution)/shard_map/all_gather | solution.py:198
  60.9 617.2 %reduce-scatter.30.cloned.1.call-start = ((), (), s32[]{:S(2)}) async-start(), calls=%async_computation.21 | async-start | bytes 5406720
  211.9 98.4 %copy-start.24 = (f32[5,3,128,64]{2,3,1,0:T(8,128)}, f32[5,3,128,64]{2,3,1,0:T(8,128)S(1)}, u32[]{:S(2)}) copy-start(f32[5,3,128,64]{2,3,1,0:T(8,128)S(1)} %get-tuple-element.331) | copy-start | bytes 1474564
  594.8 171.4 %reduce-scatter.28.cloned.1.call-start = ((), (), s32[]{:S(2)}) async-start(), calls=%async_computation.20 | async-start | bytes 5406720
  649.8 155.6 %reduce-scatter.34.cloned.1.call-start = ((), (), s32[]{:S(2)}) async-start(), calls=%async_computation.23 | async-start | bytes 921600
  679.2 89.4 %copy-start.28 = (bf16[128,2,320]{2,1,0:T(2,128)(2,1)}, bf16[128,2,320]{2,1,0:T(2,128)(2,1)S(1)}, u32[]{:S(2)}) copy-start(bf16[128,2,320]{2,1,0:T(2,128)(2,1)S(1)} %reshape.529) | copy-start | bytes 491524
  679.2 89.4 %copy-start.31 = (f32[8,8,2,128]{3,1,2,0:T(8,128)S(1)}, f32[8,8,2,128]{3,1,2,0:T(8,128)}, u32[]{:S(2)}) copy-start(f32[8,8,2,128]{3,1,2,0:T(8,128)} %copy-done.30) | copy-start | bytes 196612
  679.6 89.1 %copy-start.17 = (f32[8,8,2,128]{3,1,2,0:T(8,128)S(1)}, f32[8,8,2,128]{3,1,2,0:T(8,128)}, u32[]{:S(2)}) copy-start(f32[8,8,2,128]{3,1,2,0:T(8,128)} %copy-done.16) | copy-start | bytes 196612
  680.9 88.7 %copy-start.49 = (f32[960]{0:T(1024)S(1)}, f32[960]{0:T(1024)}, u32[]{:S(2)}) copy-start(f32[960]{0:T(1024)} %copy-done.48) | copy-start | bytes 11524
  680.9 88.7 %copy-start.58 = (f32[2,128]{1,0:T(2,128)S(1)}, f32[2,128]{1,0:T(2,128)}, u32[]{:S(2)}) copy-start(f32[2,128]{1,0:T(2,128)} %copy-done.57) | copy-start | bytes 3076
  680.9 134.6 %reduce-scatter.32.cloned.1.call-start = ((), (), s32[]{:S(2)}) async-start(), calls=%async_computation.22 | async-start | bytes 921600
  773.1 100.9 %reduce-scatter.36.cloned.1.call-start = ((), (), s32[]{:S(2)}) async-start(), calls=%async_computation.24 | async-start | bytes 6553600
  785.0 120.5 %reduce-scatter.20.cloned.1.call-start = ((), (), s32[]{:S(2)}) async-start(), calls=%async_computation.16 | async-start | bytes 2457600 | tf_op jit(solution)/shard_map/reduce_scatter | solution.py:330
  791.9 144.9 %reduce-scatter.22.cloned.1.call-start = ((), (), s32[]{:S(2)}) async-start(), calls=%async_computation.17 | async-start | bytes 2457600 | tf_op jit(solution)/shard_map/reduce_scatter | solution.py:339
  795.1 196.5 %reduce-scatter.24.cloned.1.call-start = ((), (), s32[]{:S(2)}) async-start(), calls=%async_computation.18 | async-start | bytes 6144000 | tf_op jit(solution)/shard_map/reduce_scatter | solution.py:316
  800.2 246.4 %reduce-scatter.26.cloned.1.call-start = ((), (), s32[]{:S(2)}) async-start(), calls=%async_computation.19 | async-start | bytes 6144000 | tf_op jit(solution)/shard_map/reduce_scatter | solution.py:319
  805.3 360.4 %all-reduce.10.cloned.1.call-start = ((), (), s32[]{:S(2)}) async-start(), calls=%async_computation.25 | async-start | bytes 9994240 | tf_op jit(solution)/shard_map/psum | solution.py:345
  (81 other events, 536.4 us)
Sparse Core Ops, SparseCore 0:
  9.7 38.4 all-gather.11
  50.9 51.9 all-gather.9
  105.6 51.2 all-gather.13
  158.4 29.2 all-gather.15
  189.2 54.2 all-gather.17
  245.0 54.7 all-gather.19
  301.5 54.7 all-gather.21
  594.9 83.1 reduce-scatter.29
  682.3 83.8 reduce-scatter.27
  768.5 22.4 reduce-scatter.33
  793.4 22.0 reduce-scatter.31
  817.7 56.2 reduce-scatter.35
  877.1 28.3 reduce-scatter.19
  908.4 28.3 reduce-scatter.21
  939.1 52.4 reduce-scatter.23
  994.0 52.4 reduce-scatter.25
  1051.4 114.2 all-reduce.9
where the time goes:
time: 1190 us; the launch traced here: 1180 us
  waiting for transfers between devices  449 us (38%)
  local copies, waits for them, and re-layouts  255 us (21%)
  matrix products  233 us (20%)
  blocking collectives  107 us (9%)
  other arithmetic  86 us (7%)
  loops' own time  34.1 us (3%)
  between operations  16.6 us (1%)
    dot_general x126, matrix products, product(): return jnp.einsum(form, left, right, preferred_element_type=jnp.float32)  212 us
    unnamed x22, waiting for transfers between devices  182 us
    unnamed x136, local copies, waits for them, and re-layouts  89.1 us
    psum x1, blocking collectives, local(): lax.psum(attend_shares[0].astype(jnp.bfloat16), 'ctx').astype(jnp.float32)  64.8 us
    reduce_scatter x1, waiting for transfers between devices, local(): lax.psum_scatter(up_grad.astype(jnp.bfloat16), 'fsdp', scatter_dimension=...  55 us
    reduce_scatter x1, waiting for transfers between devices, local(): lax.psum_scatter(gate_grad.astype(jnp.bfloat16), 'fsdp', scatter_dimensio...  54.8 us
    dynamic_slice x48, local copies, waits for them, and re-layouts, key_block(): lax.dynamic_slice_in_dim(sources, first_row, block_rows, 0)  52.3 us
    reduce_sum x16, other arithmetic, stats_step(): jnp.sum(jnp.exp(scores - new_top[..., None]), axis=-1)  47.1 us
  transfers between devices with their start and end apart: 17, of which 11 were waited for; matrix products, arithmetic and copies ran while one was open for 28% of the time, Pallas kernels for 0%

commit v1 on v0

v1 whole, which is shorter than its diff:
```python
import functools

import jax
import jax.numpy as jnp
import numpy as np
from jax import lax
from jax.experimental import pallas as pl
from jax.experimental.pallas import tpu as pltpu
from jax.sharding import PartitionSpec as P

D = 960
FF = 2560
HEADS = 15
KV_HEADS = 5
GROUP = 3
HEAD = 64
HALF = 64
CHUNK = 256
SIDE = 4
KV = KV_HEADS * 128
PROJ = KV + D
PART = 832
PART_AT = PROJ - PART
SHARD = D // SIDE
PADDED = 256
SLICE = FF // SIDE
EPSILON = 1e-05
THETA = 100000.0
SCALE = 0.125
MASKED = -1e30
F32 = jnp.float32
BF16 = jnp.bfloat16
NN = (((1,), (0,)), ((), ()))
NT = (((1,), (1,)), ((), ()))
TN = (((0,), (0,)), ((), ()))
LIMIT = 52 * 2**20
SMEM = pl.BlockSpec(memory_space=pltpu.SMEM)
VMEM = pl.BlockSpec(memory_space=pltpu.VMEM)


def dot(left, right, dims=NN):
    return lax.dot_general(left, right, dims, preferred_element_type=F32)


def call(kernel, name, out_shape, inputs, in_specs, scratch=()):
    return pl.pallas_call(
        kernel,
        out_shape=out_shape,
        in_specs=in_specs,
        out_specs=jax.tree.map(lambda _: VMEM, out_shape),
        scratch_shapes=list(scratch),
        compiler_params=pltpu.CompilerParams(vmem_limit_bytes=LIMIT),
        name=name,
    )(*inputs)


def ctx_index(y, x, core):
    return (y * SIDE + x) * 2 + core


def plane_pairs(step, first_turn):
    pairs = []
    for y in range(SIDE):
        for x in range(SIDE):
            for core in range(2):
                along_x = (core == 0) == first_turn
                target = (y, (x + step) % SIDE) if along_x else ((y + step) % SIDE, x)
                pairs.append((ctx_index(y, x, core), ctx_index(*target, core)))
    return pairs


def z_move(step):
    pairs = [(z, (z + step) % SIDE) for z in range(SIDE)]
    return lambda rows: lax.ppermute(rows, "fsdp", pairs)


def plane_move(step, first_turn):
    pairs = plane_pairs(step, first_turn)
    return lambda rows: lax.ppermute(rows, "ctx", pairs)


def core_swap(rows):
    pairs = [(index, index ^ 1) for index in range(2 * SIDE * SIDE)]
    return lax.ppermute(rows, "ctx", pairs)


Z_RING = (z_move(1), z_move(-1), z_move(2))
FIRST_RING = (plane_move(1, True), plane_move(-1, True), plane_move(2, True))
SECOND_RING = (plane_move(1, False), plane_move(-1, False), plane_move(2, False))


def ring_gather(rows, ring):
    plus, minus, _ = ring
    half = rows.shape[0] // 2
    before, after = plus(rows), minus(rows)
    return rows, before, after, plus(before[:half]), minus(after[half:])


def add_low(left, right):
    return (left.astype(F32) + right.astype(F32)).astype(BF16)


def ring_scatter(own, before, after, opposite_top, opposite_low, ring):
    plus, minus, _ = ring
    half = own.shape[0] // 2
    to_before, to_after = minus(opposite_top), plus(opposite_low)
    before = jnp.concatenate([add_low(before[:half], to_before), before[half:]], axis=0)
    after = jnp.concatenate([after[:half], add_low(after[half:], to_after)], axis=0)
    return own.astype(F32) + minus(before).astype(F32) + plus(after).astype(F32)


def slot_table():
    devices = 2 * SIDE * SIDE
    held = {i: [2 * i, 2 * i + 1, 2 * (i ^ 1), 2 * (i ^ 1) + 1] for i in range(devices)}
    own = {i: list(held[i]) for i in held}
    for turn in (True, False):
        source = {step: {t: s for s, t in plane_pairs(step, turn)} for step in (1, -1, 2)}
        grown = {}
        for i in held:
            half = len(held[i]) // 2
            opposite = held[source[2][i]]
            grown[i] = (
                held[i] + held[source[1][i]] + held[source[-1][i]] + opposite[:half] + opposite[half:]
            )
        held = grown
    table = np.array([held[i] for i in range(devices)], np.int32)
    assert all((table[i, :4] == own[i]).all() for i in range(devices))
    return table


def pack_kernel(core_ref, q_ref, k_ref, v_ref, gains_ref, mine_ref, other_ref):
    columns = []
    for head in range(KV_HEADS):
        at = slice(head * HEAD, (head + 1) * HEAD)
        columns += [k_ref[:, at], v_ref[:, at]]
    columns.append(q_ref[...])
    packed = jnp.concatenate(columns, axis=1)
    low, high = packed[:, :PART], packed[:, PART_AT:]
    is_low = core_ref[0] == 0
    mine_ref[:SHARD, :] = jnp.where(is_low, low, high)
    other_ref[:SHARD, :] = jnp.where(is_low, high, low)
    mine_ref[SHARD:, :] = gains_ref[...]
    other_ref[SHARD:, :] = gains_ref[...]


def rope(values, cosine, sine, back):
    lane = lax.broadcasted_iota(jnp.int32, values.shape, 1)
    first = (lane & (HEAD - 1)) < HEAD // 2
    turned = values * sine if back else values
    ahead, behind = pltpu.roll(turned, 128 - HEAD // 2, 1), pltpu.roll(turned, HEAD // 2, 1)
    if back:
        return values * cosine + jnp.where(first, ahead, -behind)
    return values * cosine + jnp.where(first, -ahead, behind) * sine


def half_tables(cosine, sine):
    lane = lax.broadcasted_iota(jnp.int32, cosine.shape, 1)
    return jnp.where(lane < HEAD, cosine, 1.0), jnp.where(lane < HEAD, sine, 0.0)


def project_kernel(
    where_ref, x_mine, x_got, cosine_ref, sine_ref, *refs
):
    pieces, (q_ref, kv_ref, normed_ref, weight_ref, gains_ref, result) = refs[:10], refs[10:]
    z, core = where_ref[0], where_ref[1]
    mine_at = pl.multiple_of(core * PART_AT, 128)
    other_at = pl.multiple_of((1 - core) * PART_AT, 128)
    gains = jnp.zeros((16, 512), F32)
    for turn, place in enumerate((z, (z + 3) & 3, (z + 1) & 3)):
        at = pl.multiple_of(place * SHARD, 16)
        for piece, column in ((pieces[2 * turn], mine_at), (pieces[2 * turn + 1], other_at)):
            weight_ref[pl.ds(at, SHARD), pl.ds(column, PART)] = piece[:SHARD, :]
        gains += pieces[2 * turn][SHARD:, :512].astype(F32)
    at = pl.multiple_of(((z + 2) & 3) * SHARD, 16)
    for top, low, column in ((pieces[6], pieces[8], mine_at), (pieces[7], pieces[9], other_at)):
        weight_ref[pl.ds(at, 128), pl.ds(column, PART)] = top[...]
        weight_ref[pl.ds(at + 128, SHARD - 128), pl.ds(column, PART)] = low[: SHARD - 128, :]
    gains += pieces[8][SHARD - 128 :, :512].astype(F32)
    wide = jnp.concatenate(
        [
            jnp.concatenate([gains[0:1], gains[1:2]], axis=1),
            jnp.concatenate([gains[2:3], gains[3:4]], axis=1),
        ],
        axis=0,
    )[:, :D]
    gains_ref[...] = wide
    rows = x_mine.shape[0]
    for half, x_ref in enumerate((x_mine, x_got)):
        x = x_ref[...].astype(F32)
        scale = lax.rsqrt(jnp.mean(x * x, axis=-1, keepdims=True) + EPSILON)
        normed_ref[half * rows : (half + 1) * rows, :] = (x * scale * wide[0:1]).astype(BF16)
    result[...] = dot(normed_ref[...], weight_ref[...])
    cosine, sine = cosine_ref[...], sine_ref[...]
    kv_tables = half_tables(cosine, sine)
    for head in range(KV_HEADS):
        at = slice(head * 128, (head + 1) * 128)
        kv_ref[:, at] = rope(result[:, at], *kv_tables, False).astype(BF16)
    for tile in range(D // 128):
        at = slice(tile * 128, (tile + 1) * 128)
        turned = rope(result[:, KV + tile * 128 : KV + (tile + 1) * 128], cosine, sine, False)
        q_ref[:, at] = (turned.astype(BF16) * SCALE).astype(BF16)
    tail = jnp.concatenate([result[:, PROJ - HEAD :]] * 2, axis=1)
    q_ref[:, D - HEAD :] = (rope(tail, cosine, sine, False)[:, :HEAD].astype(BF16) * SCALE).astype(
        BF16
    )


def sort_rows(order_ref, sources, sorted_ref):
    first = 0
    for source in sources:

        def step(slot, carry, source=source, first=first):
            place = order_ref[first + slot]
            sorted_ref[pl.ds(pl.multiple_of(place * HALF, HALF), HALF), :] = source[
                pl.ds(pl.multiple_of(slot * HALF, HALF), HALF), :
            ]
            return carry

        count = source.shape[0] // HALF
        lax.fori_loop(0, count, step, 0)
        first += count


def allowed_mask(chunk, place, rows):
    key_at = lax.broadcasted_iota(jnp.int32, (rows, CHUNK), 1) + chunk * CHUNK
    query_at = (lax.broadcasted_iota(jnp.int32, (rows, CHUNK), 0) & (HALF - 1)) + place * HALF
    return key_at <= query_at


def packed_queries(rows_ref, block, kv_head, upper):
    parts = []
    for member in range(GROUP):
        head = kv_head * GROUP + member
        part = rows_ref[block * HALF : (block + 1) * HALF, head * HEAD : (head + 1) * HEAD]
        zero = jnp.zeros_like(part)
        parts.append(jnp.concatenate([zero, part] if upper else [part, zero], axis=1))
    return jnp.concatenate(parts, axis=0)


def attend_kernel(blocks, parts, order_ref, q_ref, *refs):
    sources, (o_ref, ox_ref, lse_ref, kvs, qx, scores, tops) = refs[:parts], refs[parts:]
    rows = GROUP * HALF
    sort_rows(order_ref, sources, kvs)
    for block in range(blocks):
        for k in range(KV_HEADS):
            qx[block, k] = packed_queries(q_ref, block, k, False)

    def one_block(block, carry):
        place = order_ref[block]
        last = place >> 2
        tops[...] = jnp.full(tops.shape, MASKED, F32)

        def score_chunk(chunk, masked):
            at = pl.ds(pl.multiple_of(chunk * CHUNK, CHUNK), CHUNK)
            if masked:
                mask = allowed_mask(chunk, place, rows)
            for k in range(KV_HEADS):
                s = dot(qx[block, k], kvs[at, k * 128 : (k + 1) * 128], NT)
                if masked:
                    s = jnp.where(mask, s, MASKED)
                scores[k, chunk] = s
                tops[k] = jnp.maximum(tops[k], jnp.maximum(s[:, :128], s[:, 128:]))

        def score_step(chunk, c):
            score_chunk(chunk, False)
            return c

        lax.fori_loop(0, last, score_step, 0)
        score_chunk(last, True)
        for k in range(KV_HEADS):
            top = jnp.max(tops[k], axis=1, keepdims=True)
            tops[k] = jnp.broadcast_to(top, (rows, 128))
            lse_ref[block, k] = jnp.zeros((rows, 128), F32)
            ox_ref[block, k] = jnp.zeros((rows, 128), F32)

        def out_step(chunk, c):
            at = pl.ds(pl.multiple_of(chunk * CHUNK, CHUNK), CHUNK)
            for k in range(KV_HEADS):
                top = tops[k]
                s = scores[k, chunk]
                p0 = jnp.exp(s[:, :128] - top)
                p1 = jnp.exp(s[:, 128:] - top)
                lse_ref[block, k] += p0 + p1
                p = jnp.concatenate([p0, p1], axis=1).astype(BF16)
                ox_ref[block, k] += dot(p, kvs[at, k * 128 : (k + 1) * 128])
            return c

        lax.fori_loop(0, last + 1, out_step, 0)
        for k in range(KV_HEADS):
            total = jnp.sum(lse_ref[block, k], axis=1, keepdims=True)
            ox_ref[block, k] = ox_ref[block, k] / total
            lse_ref[block, k] = tops[k] + jnp.log(total)
        return carry

    lax.fori_loop(0, blocks, one_block, 0)
    for block in range(blocks):
        pieces = [
            ox_ref[block, k, g * HALF : (g + 1) * HALF, HEAD:].astype(BF16)
            for k in range(KV_HEADS)
            for g in range(GROUP)
        ]
        o_ref[block * HALF : (block + 1) * HALF, :] = jnp.concatenate(pieces, axis=1)


def attend(order, q, sources):
    length = sum(source.shape[0] for source in sources)
    blocks = q.shape[0] // HALF
    rows = GROUP * HALF
    packed = jax.ShapeDtypeStruct((blocks, KV_HEADS, rows, 128), F32)
    return call(
        functools.partial(attend_kernel, blocks, len(sources)),
        "attend",
        (jax.ShapeDtypeStruct(q.shape, BF16), packed, packed),
        (order, q, *sources),
        [SMEM] + [VMEM] * (1 + len(sources)),
        [
            pltpu.VMEM((length, KV), BF16),
            pltpu.VMEM((blocks, KV_HEADS, rows, 128), BF16),
            pltpu.VMEM((KV_HEADS, length // CHUNK, rows, CHUNK), F32),
            pltpu.VMEM((KV_HEADS, rows, 128), F32),
        ],
    )


def attend_back_kernel(blocks, parts, order_ref, q_ref, g_ref, ox_ref, lse_ref, *refs):
    sources, refs = refs[:parts], refs[parts:]
    dq_ref, refs = refs[0], refs[1:]
    results, (kvs, qg, qgt, dots, dqx, dkvt) = refs[:parts], refs[parts:]
    rows = GROUP * HALF
    sort_rows(order_ref, sources, kvs)
    for block in range(blocks):
        for k in range(KV_HEADS):
            q = packed_queries(q_ref, block, k, False)
            g = packed_queries(g_ref, block, k, True)
            qg[block, k, :rows, :] = q
            qg[block, k, rows:, :] = g
            both = jnp.concatenate([q, g], axis=0).astype(F32)
            qgt[block, k] = both.T.astype(BF16)
            summed = jnp.sum(g.astype(F32) * ox_ref[block, k], axis=1, keepdims=True)
            dots[block, k] = jnp.broadcast_to(summed, (rows, 128))
    dqx[...] = jnp.zeros(dqx.shape, F32)

    def clear(chunk, c):
        dkvt[chunk] = jnp.zeros(dkvt.shape[1:], F32)
        return c

    lax.fori_loop(0, dkvt.shape[0], clear, 0)

    def one_block(block, carry):
        place = order_ref[block]
        last = place >> 2

        def chunk_work(chunk, masked):
            at = pl.ds(pl.multiple_of(chunk * CHUNK, CHUNK), CHUNK)
            if masked:
                mask = allowed_mask(chunk, place, rows)
            for k in range(KV_HEADS):
                keys = kvs[at, k * 128 : (k + 1) * 128]
                both = dot(qg[block, k], keys, NT)
                lse = lse_ref[block, k]
                dots_here = dots[block, k]
                ps, ds = [], []
                for half in range(2):
                    lanes = slice(half * 128, (half + 1) * 128)
                    p = jnp.exp(both[:rows, lanes] - lse)
                    if masked:
                        p = jnp.where(mask[:, lanes], p, 0.0)
                    ps.append(p.astype(BF16))
                    ds.append((p * (both[rows:, lanes] - dots_here)).astype(BF16))
                p = jnp.concatenate(ps, axis=1)
                d = jnp.concatenate(ds, axis=1)
                dqx[block, k] += dot(d, keys)
                dkvt[chunk, k] += dot(qgt[block, k], jnp.concatenate([d, p], axis=0))

        def step(chunk, c):
            chunk_work(chunk, False)
            return c

        lax.fori_loop(0, last, step, 0)
        chunk_work(last, True)
        return carry

    lax.fori_loop(0, blocks, one_block, 0)
    for block in range(blocks):
        pieces = [
            dqx[block, k, g * HALF : (g + 1) * HALF, :HEAD] * SCALE
            for k in range(KV_HEADS)
            for g in range(GROUP)
        ]
        dq_ref[block * HALF : (block + 1) * HALF, :] = jnp.concatenate(pieces, axis=1)

    def turn(chunk, c):
        at = pl.ds(pl.multiple_of(chunk * CHUNK, CHUNK), CHUNK)
        for k in range(KV_HEADS):
            kvs[at, k * 128 : (k + 1) * 128] = dkvt[chunk, k].T.astype(BF16)
        return c

    lax.fori_loop(0, dkvt.shape[0], turn, 0)
    first = 0
    for result in results:

        def unsort(slot, c, result=result, first=first):
            place = order_ref[first + slot]
            result[pl.ds(pl.multiple_of(slot * HALF, HALF), HALF), :] = kvs[
                pl.ds(pl.multiple_of(place * HALF, HALF), HALF), :
            ]
            return c

        count = result.shape[0] // HALF
        lax.fori_loop(0, count, unsort, 0)
        first += count


def attend_back(order, q, g, ox, lse, sources):
    length = sum(source.shape[0] for source in sources)
    blocks = q.shape[0] // HALF
    rows = GROUP * HALF
    return call(
        functools.partial(attend_back_kernel, blocks, len(sources)),
        "attend_back",
        (jax.ShapeDtypeStruct(q.shape, F32),)
        + tuple(jax.ShapeDtypeStruct(source.shape, BF16) for source in sources),
        (order, q, g, ox, lse, *sources),
        [SMEM] + [VMEM] * (4 + len(sources)),
        [
            pltpu.VMEM((length, KV), BF16),
            pltpu.VMEM((blocks, KV_HEADS, 2 * rows, 128), BF16),
            pltpu.VMEM((blocks, KV_HEADS, 128, 2 * rows), BF16),
            pltpu.VMEM((blocks, KV_HEADS, rows, 128), F32),
            pltpu.VMEM((blocks, KV_HEADS, rows, 128), F32),
            pltpu.VMEM((length // CHUNK, KV_HEADS, 128, CHUNK), F32),
        ],
    )


def query_back_kernel(dq_ref, cosine_ref, sine_ref, low_ref):
    cosine, sine = cosine_ref[...], sine_ref[...]
    for tile in range(D // 128):
        at = slice(tile * 128, (tile + 1) * 128)
        low_ref[:, at] = rope(dq_ref[:, at], cosine, sine, True).astype(BF16)
    tail = jnp.concatenate([dq_ref[:, D - HEAD :]] * 2, axis=1)
    low_ref[:, D - HEAD :] = rope(tail, cosine, sine, True)[:, :HEAD].astype(BF16)


def input_back_kernel(
    x_mine, x_got, dkv_ref, q_low_ref, cosine_ref, sine_ref, weight_ref, gains_ref, middle_ref,
    low_ref, grads_ref, gain_ref,
):
    kv_tables = half_tables(cosine_ref[...], sine_ref[...])
    for head in range(KV_HEADS):
        at = slice(head * 128, (head + 1) * 128)
        low_ref[:, at] = rope(dkv_ref[:, at], *kv_tables, True).astype(BF16)
    low_ref[:, KV:] = q_low_ref[...]
    back = dot(low_ref[...], weight_ref[...], NT)
    rows = x_mine.shape[0]
    gain = gains_ref[0:1, :]
    total = jnp.zeros((1, D), F32)
    for half, x_ref in enumerate((x_mine, x_got)):
        at = slice(half * rows, (half + 1) * rows)
        x = x_ref[...].astype(F32)
        scale = lax.rsqrt(jnp.mean(x * x, axis=-1, keepdims=True) + EPSILON)
        unit = x * scale
        total += jnp.sum(back[at] * unit, axis=0, keepdims=True)
        weighted = back[at] * gain
        inner = jnp.mean(weighted * unit, axis=-1, keepdims=True)
        grads_ref[at, :] = middle_ref[at, :] + scale * (weighted - unit * inner)
    gain_ref[...] = total


def rope_tables(places):
    pair_ids = jnp.arange(HEAD // 2, dtype=F32)
    frequency = THETA ** (-2.0 * pair_ids / HEAD)
    angles = places.astype(F32)[:, None] * frequency[None, :]
    return jnp.tile(jnp.cos(angles), (1, 4)), jnp.tile(jnp.sin(angles), (1, 4))


def norm_back(grad_normed, values, scale, gain):
    unit_rows = values * scale
    gain_grad = jnp.sum(grad_normed * unit_rows, axis=0)
    weighted = grad_normed * gain
    inner = jnp.mean(weighted * unit_rows, axis=-1, keepdims=True)
    return gain_grad, scale * (weighted - unit_rows * inner)


def after(value, *others):
    return lax.optimization_barrier((value, *others))[0]


def rows_at(array, block, size):
    return lax.dynamic_slice_in_dim(array, block * size, size, 0)


def assemble(pieces, places, axis):
    size = pieces[0].shape[axis]
    shape = list(pieces[0].shape)
    shape[axis] = size * len(pieces)
    whole = jnp.zeros(shape, pieces[0].dtype)
    for piece, place in zip(pieces, places):
        whole = lax.dynamic_update_slice_in_dim(whole, piece, place * size, axis)
    return whole


def local(
    activations, cotangent, block_order, attend_gain, query_weight, key_weight, value_weight,
    output_weight, dense_gain, gate_weight, up_weight, down_weight,
):
    index = lax.axis_index("ctx")
    z = lax.axis_index("fsdp")
    core = index & 1
    tokens = activations.shape[1]
    rows = 2 * tokens
    ring_places = (z, (z + 3) & 3, (z + 1) & 3, (z + 2) & 3)

    x_mine = lax.dynamic_index_in_dim(activations, core, 0, False)
    x_got = core_swap(lax.dynamic_index_in_dim(activations, 1 - core, 0, False))

    gains = jnp.stack(
        [
            lax.dynamic_update_slice_in_dim(jnp.zeros((1024,), BF16), gain, z * SHARD, 0)
            for gain in (attend_gain, dense_gain)
        ]
    ).reshape(4, 512)
    gains = jnp.pad(gains, ((0, 12), (0, PART - 512)))
    shape = jax.ShapeDtypeStruct((PADDED, PART), BF16)
    mine, other = call(
        pack_kernel, "pack", (shape, shape),
        (core.reshape(1).astype(jnp.int32), query_weight, key_weight, value_weight, gains),
        [SMEM] + [VMEM] * 4,
    )
    ringed = ring_gather(mine, Z_RING)
    pieces = [mine, other]
    for piece in ringed[1:]:
        pieces += [piece, core_swap(piece)]

    slots = jnp.asarray(slot_table())[index]
    order = jnp.sum(
        jnp.where(slots[:, None] == jnp.arange(64, dtype=jnp.int32)[None, :], block_order[None, :], 0),
        axis=1,
    )
    places = (order[: rows // HALF, None] * HALF + jnp.arange(HALF, dtype=jnp.int32)).reshape(rows)
    cosine, sine = rope_tables(places)
    queries, kv, normed_one, weight, gain_rows = call(
        project_kernel,
        "project",
        (
            jax.ShapeDtypeStruct((rows, D), BF16),
            jax.ShapeDtypeStruct((rows, KV), BF16),
            jax.ShapeDtypeStruct((rows, D), BF16),
            jax.ShapeDtypeStruct((D, PROJ), BF16),
            jax.ShapeDtypeStruct((2, D), F32),
        ),
        (jnp.stack([z, core]).astype(jnp.int32), x_mine, x_got, cosine, sine, *pieces),
        [SMEM] + [VMEM] * 14,
        [pltpu.VMEM((rows, PROJ), F32)],
    )

    line = jnp.concatenate(ring_gather(kv, FIRST_RING), axis=0)
    sources = ring_gather(line, SECOND_RING)

    cotangent, output_weight, gate_weight, up_weight = lax.optimization_barrier(
        (cotangent, output_weight, gate_weight, up_weight, kv)
    )[:4]
    wo = lax.all_gather(output_weight, "fsdp", axis=0, tiled=True)
    g_mine = lax.dynamic_index_in_dim(cotangent, core, 0, False)
    g_got = core_swap(lax.dynamic_index_in_dim(cotangent, 1 - core, 0, False))
    g_own = jnp.concatenate([g_mine, g_got], axis=0)
    g_rows = jnp.concatenate(ring_gather(g_own, Z_RING), axis=0)

    def columns_for(place):
        return jnp.concatenate(
            [
                lax.dynamic_slice_in_dim(w, place * SLICE, SLICE, 1)
                for w in (gate_weight, up_weight)
            ],
            axis=1,
        )

    came = (
        columns_for(z),
        Z_RING[0](columns_for((z + 1) & 3)),
        Z_RING[1](columns_for((z + 3) & 3)),
        Z_RING[2](columns_for((z + 2) & 3)),
    )
    gate_up = assemble(came, ring_places, 0)
    normed_swapped = core_swap(normed_one)

    attended, ox, lse = attend(order, queries, sources)

    x = jnp.concatenate([x_mine, x_got], axis=0).astype(F32)
    middle = x + dot(attended, wo)
    gain_two = gain_rows[1]
    scale_two = lax.rsqrt(jnp.mean(middle * middle, axis=-1, keepdims=True) + EPSILON)
    normed_two = (middle * scale_two * gain_two).astype(BF16)

    n_rows = jnp.concatenate(ring_gather(normed_two, Z_RING), axis=0)
    gate_rows = dot(n_rows, gate_up[:, :SLICE])
    upper = dot(n_rows, gate_up[:, SLICE:])
    sigmoid_gate = jax.nn.sigmoid(gate_rows)
    hidden = (gate_rows * sigmoid_gate * upper).astype(BF16)
    grad_hidden = dot(g_rows, down_weight, NT)
    grad_gate = (
        grad_hidden * upper * sigmoid_gate * (1.0 + gate_rows * (1.0 - sigmoid_gate))
    ).astype(BF16)
    grad_upper = (grad_hidden * gate_rows * sigmoid_gate).astype(BF16)
    grad_both = jnp.concatenate([grad_gate, grad_upper], axis=1)
    grad_normed = dot(grad_both, gate_up, NT).astype(BF16)

    def split(array):
        half = rows // 2
        cuts = [0, rows, 2 * rows, 3 * rows, 3 * rows + half, 4 * rows]
        return [array[a:b] for a, b in zip(cuts[:-1], cuts[1:])]

    grad_normed_two = ring_scatter(*split(grad_normed), Z_RING)
    dense_gain_grad, norm_two_back = norm_back(grad_normed_two, middle, scale_two, gain_two)
    grad_middle = g_own.astype(F32) + norm_two_back
    grad_branch = grad_middle.astype(BF16)
    grad_attended = dot(grad_branch, wo, NT).astype(BF16)

    dq, *dkv = attend_back(order, queries, grad_attended, ox, lse, sources)

    low_grad_attended = grad_attended
    hidden, n_rows, grad_both = after((hidden, n_rows, grad_both), low_grad_attended)
    down_rows = dot(hidden, down_weight).astype(BF16)
    down_grad = dot(hidden, g_rows, TN).astype(BF16)
    both_grad = dot(n_rows, grad_both, TN).astype(BF16)
    output_grad = dot(attended, grad_branch, TN).astype(BF16)
    came = (
        rows_at(both_grad, z, SHARD),
        Z_RING[0](rows_at(both_grad, (z + 1) & 3, SHARD)),
        Z_RING[1](rows_at(both_grad, (z + 3) & 3, SHARD)),
        Z_RING[2](rows_at(both_grad, (z + 2) & 3, SHARD)),
    )
    gate_grad = assemble([piece[:, :SLICE] for piece in came], ring_places, 1)
    up_grad = assemble([piece[:, SLICE:] for piece in came], ring_places, 1)
    blocks = [rows_at(output_grad, place, SHARD) for place in ring_places]
    output_grad = ring_scatter(
        *blocks[:3], blocks[3][: SHARD // 2], blocks[3][SHARD // 2 :], Z_RING
    ).astype(BF16)
    dense_grads = lax.psum((output_grad, gate_grad, up_grad, down_grad), "ctx")
    layer_rows = (middle + ring_scatter(*split(down_rows), Z_RING)).astype(BF16)

    line = ring_scatter(*dkv, SECOND_RING).astype(BF16)
    dkv_own = ring_scatter(*split(line), FIRST_RING)
    q_low = call(
        query_back_kernel, "query_back", jax.ShapeDtypeStruct((rows, D), BF16),
        (dq, cosine, sine), [VMEM] * 3,
    )
    low, input_rows, attend_gain_grad = call(
        input_back_kernel,
        "input_back",
        (
            jax.ShapeDtypeStruct((rows, PROJ), BF16),
            jax.ShapeDtypeStruct((rows, D), F32),
            jax.ShapeDtypeStruct((1, D), F32),
        ),
        (x_mine, x_got, dkv_own, q_low, cosine, sine, weight, gain_rows, grad_middle),
        [VMEM] * 9,
    )

    mine_at, other_at = core * PART_AT, (1 - core) * PART_AT
    low_mine = lax.dynamic_slice_in_dim(low, mine_at, PART, 1)
    low_got = core_swap(lax.dynamic_slice_in_dim(low, other_at, PART, 1))
    part_grad = dot(normed_one, low_mine, TN) + dot(normed_swapped, low_got, TN)
    gain_grads = jnp.concatenate([attend_gain_grad, dense_gain_grad[None, :]], axis=0)

    def part_for(place):
        row = lax.dynamic_slice_in_dim(gain_grads, place * SHARD, SHARD, 1)
        row = jnp.pad(row, ((0, PADDED - SHARD - 2), (0, PART - SHARD)))
        return jnp.concatenate([rows_at(part_grad, place, SHARD), row], axis=0).astype(BF16)

    blocks = [part_for(place) for place in ring_places]
    part = ring_scatter(*blocks[:3], blocks[3][:128], blocks[3][128:], Z_RING).astype(BF16)
    y, x_at = index >> 3, (index >> 1) & 3
    first_place = jnp.where(core == 0, x_at, y)
    quarters = [rows_at(part, (first_place + step) & 3, PADDED // 4) for step in (0, 3, 1, 2)]
    quarter = ring_scatter(*quarters[:3], quarters[3][:32], quarters[3][32:], FIRST_RING).astype(BF16)
    quarter_sum = quarter.astype(F32)
    for move in SECOND_RING:
        quarter_sum += move(quarter).astype(F32)
    quarter = quarter_sum.astype(BF16)
    part = assemble(
        [quarter] + [move(quarter) for move in FIRST_RING],
        [(first_place + step) & 3 for step in (0, 3, 1, 2)],
        0,
    )
    part_got = core_swap(part)
    is_low = core == 0
    low_part = jnp.where(is_low, part, part_got)
    high_part = jnp.where(is_low, part_got, part)
    gain_total = part[SHARD : SHARD + 2, :SHARD].astype(F32) + part_got[SHARD : SHARD + 2, :SHARD].astype(F32)
    kv_grad = low_part[:SHARD, :KV].astype(F32).reshape(SHARD, KV_HEADS, 2, HEAD)
    query_grad = jnp.concatenate(
        [low_part[:SHARD, KV:PART], high_part[:SHARD, PART - PART_AT :]], axis=1
    ).astype(F32)

    def back_to_cores(array):
        keep, give = array[:tokens], array[tokens:]
        got = core_swap(give)
        return jnp.where(is_low, jnp.stack([keep, got]), jnp.stack([got, keep]))

    output_grad, gate_grad, up_grad, down_grad = dense_grads
    return (
        back_to_cores(layer_rows),
        back_to_cores(input_rows.astype(BF16)).astype(F32),
        gain_total[0],
        query_grad,
        kv_grad[:, :, 0].reshape(SHARD, KV_HEADS * HEAD),
        kv_grad[:, :, 1].reshape(SHARD, KV_HEADS * HEAD),
        output_grad.astype(F32),
        gain_total[1],
        gate_grad.astype(F32),
        up_grad.astype(F32),
        down_grad.astype(F32),
    )


def solution(mesh):
    tokens = P("fsdp", "ctx", None)
    gain, weight = P("fsdp"), P("fsdp", None)
    weights = (gain, weight, weight, weight, weight, gain, weight, weight, weight)
    return jax.shard_map(
        local,
        mesh=mesh,
        in_specs=(tokens, tokens, P()) + weights,
        out_specs=(tokens, tokens) + weights,
        check_vma=False,
    )
```

time: 1190 us -> 540 us (0.45)
  waiting for transfers between devices: 449 us -> 161 us
  matrix products: 233 us -> 30.6 us
  local copies, waits for them, and re-layouts: 255 us -> 68.8 us
  starting transfers between devices: 1.07 us -> 124 us
  blocking collectives: 107 us -> 0 us
  Pallas kernels: 0 us -> 85.3 us
  other arithmetic: 86 us -> 44.8 us
  loops' own time: 34.1 us -> 0 us
    dot_general x133 -> x12, matrix products: 233 us -> 30.6 us  [dot(): return lax.dot_general(left, right, dims, preferred_element_type=F32)]
    unnamed x22 -> x2, waiting for transfers between devices: 182 us -> 0.03 us
    reduce_scatter x4 -> x0, waiting for transfers between devices: 170 us -> none  [the longest x1 55 us: local(): lax.psum_scatter(up_grad.astype(jnp.bfloat16), 'fsdp', scatter_dimension=...]
    ppermute x0 -> x71, starting transfers between devices: none -> 124 us  [the longest x34 46.2 us: z_move(): return lambda rows: lax.ppermute(rows, 'fsdp', pairs)]
    ppermute x0 -> x71, waiting for transfers between devices: none -> 101 us  [the longest x34 64.7 us: z_move(): return lambda rows: lax.ppermute(rows, 'fsdp', pairs)]
    pallas_call x0 -> x6, Pallas kernels: none -> 85.3 us  [call(): pl.pallas_call(kernel, out_shape=out_shape, in_specs=in_specs, out_specs=...]
    dynamic_slice x144 -> x9, local copies, waits for them, and re-layouts: 95 us -> 12 us  [the longest x2 3.65 us: local(): g_got = core_swap(lax.dynamic_index_in_dim(cotangent, 1 - core, 0, False))]
    unnamed x136 -> x119, local copies, waits for them, and re-layouts: 89.1 us -> 20.3 us
  transfers between devices with their start and end apart: 17 -> 73, of which waited for: 11 -> 30; matrix products, arithmetic and copies ran while one was open for 28% -> 21% of each run, Pallas kernels for 0% -> 15%
where the time goes in v1:
time: 540 us; the launch traced here: 530 us
  waiting for transfers between devices  161 us (30%)
  starting transfers between devices  124 us (23%)
  Pallas kernels  85.3 us (16%)
  local copies, waits for them, and re-layouts  68.8 us (13%)
  other arithmetic  44.8 us (8%)
  matrix products  30.6 us (6%)
  between operations  15.5 us (3%)
    pallas_call x6, Pallas kernels, call(): pl.pallas_call(kernel, out_shape=out_shape, in_specs=in_specs, out_specs=...  85.3 us
    ppermute x34, waiting for transfers between devices, z_move(): return lambda rows: lax.ppermute(rows, 'fsdp', pairs)  64.7 us
    psum x1, waiting for transfers between devices, local(): dense_grads = lax.psum((output_grad, gate_grad, up_grad, down_grad), 'ctx')  60 us
    ppermute x34, starting transfers between devices, z_move(): return lambda rows: lax.ppermute(rows, 'fsdp', pairs)  46.2 us
    ppermute x11, starting transfers between devices, core_swap(): return lax.ppermute(rows, 'ctx', pairs)  45.9 us
    ppermute x26, waiting for transfers between devices, plane_move(): return lambda rows: lax.ppermute(rows, 'ctx', pairs)  36.3 us
    ppermute x26, starting transfers between devices, plane_move(): return lambda rows: lax.ppermute(rows, 'ctx', pairs)  31.5 us
    dot_general x12, matrix products, dot(): return lax.dot_general(left, right, dims, preferred_element_type=F32)  30.6 us
  transfers between devices with their start and end apart: 73, of which 30 were waited for; matrix products, arithmetic and copies ran while one was open for 21% of the time, Pallas kernels for 15%

profile of v1, /device:TPU:1, one launch (start us, length us, event | category | flops | bytes accessed | tf_op | source)
XLA Modules:
  0.0 529.7 jit_solution(17685484358881284576)
XLA Ops:
  21.8 6.6 %collective-permute-done.1.refs_2_ = bf16[256,832]{1,0:T(8,128)(2,1)} collective-permute-done((bf16[256,832]{1,0:T(8,128)(2,1)S(1)}, bf16[256,832]{1,0:T(8,128)(2,1)}, u32[]{:S(2)}, u32[]{:S(2)}) %collective-permute-start.1) | collective-permute-done | bytes 426016 | tf_op jit(solution)/shard_map/ppermute | solution.py:74
  41.0 4.6 project.1
  92.7 5.8 %collective-permute-done.23 = bf16[240,1280]{1,0:T(8,128)(2,1)S(1)} collective-permute-done((bf16[240,1280]{1,0:T(8,128)(2,1)}, bf16[240,1280]{1,0:T(8,128)(2,1)S(1)}, u32[]{:S(2)}, u32[]{:S(2)}) %collective-permute-start.23) | collective-permute-done | bytes 614432 | tf_op jit(solution)/shard_map/ppermute | solution.py:74
  99.3 9.2 %collective-permute-done.25 = bf16[256,960]{1,0:T(8,128)(2,1)S(1)} collective-permute-done((bf16[256,960]{1,0:T(8,128)(2,1)S(1)}, bf16[256,960]{1,0:T(8,128)(2,1)S(1)}, u32[]{:S(2)}, u32[]{:S(2)}) %collective-permute-start.25) | collective-permute-done | bytes 491552 | tf_op jit(solution)/shard_map/ppermute | solution.py:74
  109.5 3.4 collective-permute-start.28
  113.0 3.9 collective-permute-done.27
  119.1 27.3 %attend.1 = (bf16[256,960]{1,0:T(8,128)(2,1)S(1)}, f32[4,5,192,128]{3,2,1,0:T(8,128)}, f32[4,5,192,128]{3,2,1,0:T(8,128)}) custom-call(s32[64]{0:T(128)S(1)} %select_reduce_fusion.order_ref, bf16[256,960]{1,0:T(8,128)(2,1)S(1)} %copy-done.2, bf16[1024,640]{1,0:T(8,128)(2,1)} %constant_dynamic-update-slice_fusion.refs_0_, bf16[1024,640]{1,0:T(8,128)(2,1)} %copy-done.13, ...), custom_call_target="tpu_custom_call" | custom-call | tf_op jit(solution)/shard_map/attend/pallas_call | solution.py:46
  155.4 8.6 %collective-permute-done.17 = bf16[256,960]{1,0:T(8,128)(2,1)S(1)} collective-permute-done((bf16[256,960]{1,0:T(8,128)(2,1)S(1)}, bf16[256,960]{1,0:T(8,128)(2,1)S(1)}, u32[]{:S(2)}, u32[]{:S(2)}) %collective-permute-start.17) | collective-permute-done | bytes 491552 | tf_op jit(solution)/shard_map/ppermute | solution.py:74
  170.7 3.7 fusion
  174.4 5.1 multiply_convert_fusion.1
  179.5 5.8 %convolution_convert_fusion.1 = bf16[1024,960]{1,0:T(8,128)(2,1)S(1)} fusion(bf16[960,1280]{1,0:T(8,128)(2,1)} %constant_dynamic-update-slice_fusion.16, bf16[1024,640]{0,1:T(8,128)(2,1)S(1)} %get-tuple-element.121, bf16[1024,640]{0,1:T(8,128)(2,1)S(1)} %get-tuple-element.119), kind=kOutput, calls=%fused_computation.8 | convolution fusion | flops 2522808320 | bytes 7045120 | tf_op jit(solution)/shard_map/dot_general | solution.py:42
  198.4 6.2 %collective-permute-start.47 = (bf16[256,960]{1,0:T(8,128)(2,1)}, bf16[256,960]{1,0:T(8,128)(2,1)}, u32[]{:S(2)}, u32[]{:S(2)}) collective-permute-start(bf16[256,960]{1,0:T(8,128)(2,1)} %get-tuple-element.58), channel_id=1, source_target_pairs={{0,4},{4,0},{8,12},{12,8},{16,20},{20,16},{24,28},{28,24},{32,36},... | collective-permute-start | bytes 1474568 | tf_op jit(solution)/shard_map/ppermute | solution.py:84
  210.7 47.6 %attend_back.1 = (f32[256,960]{1,0:T(8,128)}, bf16[1024,640]{1,0:T(8,128)(2,1)}, bf16[1024,640]{1,0:T(8,128)(2,1)}, bf16[1024,640]{1,0:T(8,128)(2,1)}, bf16[512,...) custom-call(s32[64]{0:T(128)S(1)} %select_reduce_fusion.order_ref, bf16[256,960]{1,0:T(8,128)(2,1)S(1)} %copy-done.2, ...), custom_call_target="tpu_custom_call" | custom-call | tf_op jit(solution)/shard_map/attend_back/pallas_call | solution.py:46
  268.6 3.4 collective-permute-start.39
  280.0 6.5 %collective-permute-done.39 = bf16[1024,640]{1,0:T(8,128)(2,1)S(1)} collective-permute-done((bf16[1024,640]{1,0:T(8,128)(2,1)S(1)}, bf16[1024,640]{1,0:T(8,128)(2,1)S(1)}, u32[]{:S(2)}, u32[]{:S(2)}) %collective-permute-start.39) | collective-permute-done | bytes 1310752 | tf_op jit(solution)/shard_map/ppermute | solution.py:79
  286.5 3.8 collective-permute-done.41
  313.8 4.9 input_back.1
  321.9 14.7 %collective-permute-start.48 = (bf16[256,832]{1,0:T(8,128)(2,1)}, bf16[256,832]{1,0:T(8,128)(2,1)S(1)}, u32[]{:S(2)}, u32[]{:S(2)}) collective-permute-start(bf16[256,832]{1,0:T(8,128)(2,1)} %constant_dynamic-slice_fusion.18), channel_id=1, source_target_pairs={{0,4},{4,0},{8,12},{12,8},{16,20},{20,16},{24,28},{28,24},{32,36},... | collective-permute-start | bytes 1277960 | tf_op jit(solution)/shard_map/ppermute | solution.py:84
  351.7 8.7 %collective-permute-done.49 = bf16[128,832]{0,1:T(8,128)(2,1)S(1)} collective-permute-done((bf16[128,832]{0,1:T(8,128)(2,1)}, bf16[128,832]{0,1:T(8,128)(2,1)S(1)}, u32[]{:S(2)}, u32[]{:S(2)}) %collective-permute-start.49) | collective-permute-done | bytes 213024 | tf_op jit(solution)/shard_map/ppermute | solution.py:74
  363.6 4.8 collective-permute-done.51
  378.2 3.8 collective-permute-done.52
  405.6 8.4 %collective-permute-done.57 = bf16[64,832]{0,1:T(8,128)(2,1)S(1)} collective-permute-done((bf16[64,832]{0,1:T(8,128)(2,1)S(1)}, bf16[64,832]{0,1:T(8,128)(2,1)S(1)}, u32[]{:S(2)}, u32[]{:S(2)}) %collective-permute-start.57) | collective-permute-done | bytes 106528 | tf_op jit(solution)/shard_map/ppermute | solution.py:79
  417.1 16.7 %collective-permute-start.37 = (bf16[128,960]{1,0:T(8,128)(2,1)S(1)}, bf16[128,960]{1,0:T(8,128)(2,1)}, u32[]{:S(2)}, u32[]{:S(2)}) collective-permute-start(bf16[128,960]{1,0:T(8,128)(2,1)S(1)} %get-tuple-element.170), channel_id=1, source_target_pairs={{0,4},{4,0},{8,12},{12,8},{16,20},{20,16},{24,28},{28,24},{32,36},... | collective-permute-start | bytes 737288 | tf_op jit(solution)/shard_map/ppermute | solution.py:84
  450.4 60.0 %all-reduce.8.cloned.1.call-done = (bf16[240,960]{1,0:T(8,128)(2,1)}, bf16[240,2560]{1,0:T(8,128)(2,1)}, bf16[240,2560]{1,0:T(8,128)(2,1)}, bf16[640,960]{0,1:T(8,128)(2,1)}) async-done(((bf16[240,960]{1,0:T(8,128)(2,1)}, bf16[240,2560]{1,0:T(8,128)(2,1)}, bf16[240,2560]{1,0:T(8,128)(2,1)}, bf16[640,960]{0,1:T(8,128)(2,1)}), (bf16[240,960]{1,0:T(8,128)(2,1)}, bf16[240,2560]{1,0:T(8,128)(2,1)}, ...) | async-done | bytes 4147216 | tf_op jit(solution)/shard_map/psum | solution.py:639
  (391 shorter events, 240.9 us)
Async XLA Ops:
  7.2 140.0 %all-gather.2.cloned.1.call-start = ((), (), s32[]{:S(2)}) async-start(), calls=%async_computation | async-start | bytes 2457600 | tf_op jit(solution)/shard_map/all_gather | solution.py:563
  50.4 31.3 %collective-permute-start.21 = (bf16[240,1280]{1,0:T(8,128)(2,1)}, bf16[240,1280]{1,0:T(8,128)(2,1)}, u32[]{:S(2)}, u32[]{:S(2)}) collective-permute-start(bf16[240,1280]{1,0:T(8,128)(2,1)} %pad_maximum_fusion.3), channel_id=1, source_target_pairs={{0,1},{1,2},{2,3},{3,0},{4,5},{5,6},{6,7},{7,4},{8,9},{9,10},{10,1... | collective-permute-start | bytes 1843208 | tf_op jit(solution)/shard_map/ppermute | solution.py:74
  51.5 36.5 %collective-permute-start.22 = (bf16[240,1280]{1,0:T(8,128)(2,1)}, bf16[240,1280]{1,0:T(8,128)(2,1)}, u32[]{:S(2)}, u32[]{:S(2)}) collective-permute-start(bf16[240,1280]{1,0:T(8,128)(2,1)} %pad_maximum_fusion.4), channel_id=1, source_target_pairs={{0,3},{1,0},{2,1},{3,2},{4,7},{5,4},{6,5},{7,6},{8,11},{9,8},{10,9... | collective-permute-start | bytes 1843208 | tf_op jit(solution)/shard_map/ppermute | solution.py:74
  54.8 455.6 %all-reduce.8.cloned.1.call-start = ((), (), s32[]{:S(2)}) async-start(), calls=%async_computation.1 | async-start | bytes 8355840 | tf_op jit(solution)/shard_map/psum | solution.py:639
  62.8 22.3 %collective-permute-start.13 = (bf16[1024,640]{1,0:T(8,128)(2,1)}, bf16[1024,640]{1,0:T(8,128)(2,1)S(1)}, u32[]{:S(2)}, u32[]{:S(2)}) collective-permute-start(bf16[1024,640]{1,0:T(8,128)(2,1)} %constant_dynamic-update-slice_fusion.refs_0_), channel_id=1, source_target_pairs={{0,32},{4,12},{8,40},{12,20},{16,48},{20,28},{24,56},{28,4},{32,64... | collective-permute-start | bytes 3932168 | tf_op jit(solution)/shard_map/ppermute | solution.py:79
  64.0 22.7 %collective-permute-start.14 = (bf16[1024,640]{1,0:T(8,128)(2,1)}, bf16[1024,640]{1,0:T(8,128)(2,1)}, u32[]{:S(2)}, u32[]{:S(2)}) collective-permute-start(bf16[1024,640]{1,0:T(8,128)(2,1)} %constant_dynamic-update-slice_fusion.refs_0_), channel_id=1, source_target_pairs={{0,96},{4,28},{8,104},{12,4},{16,112},{20,12},{24,120},{28,20},{32... | collective-permute-start | bytes 3932168 | tf_op jit(solution)/shard_map/ppermute | solution.py:79
  81.7 26.8 %collective-permute-start.25 = (bf16[256,960]{1,0:T(8,128)(2,1)S(1)}, bf16[256,960]{1,0:T(8,128)(2,1)S(1)}, u32[]{:S(2)}, u32[]{:S(2)}) collective-permute-start(bf16[256,960]{1,0:T(8,128)(2,1)S(1)} %pad_maximum_fusion.6), channel_id=1, source_target_pairs={{0,1},{1,2},{2,3},{3,0},{4,5},{5,6},{6,7},{7,4},{8,9},{9,10},{10,1... | collective-permute-start | bytes 1474568 | tf_op jit(solution)/shard_map/ppermute | solution.py:74
  85.1 23.7 %collective-permute-start.26 = (bf16[256,960]{1,0:T(8,128)(2,1)S(1)}, bf16[256,960]{1,0:T(8,128)(2,1)S(1)}, u32[]{:S(2)}, u32[]{:S(2)}) collective-permute-start(bf16[256,960]{1,0:T(8,128)(2,1)S(1)} %pad_maximum_fusion.6), channel_id=1, source_target_pairs={{0,3},{1,0},{2,1},{3,2},{4,7},{5,4},{6,5},{7,6},{8,11},{9,8},{10,9... | collective-permute-start | bytes 1474568 | tf_op jit(solution)/shard_map/ppermute | solution.py:74
  86.8 30.2 %collective-permute-start.15 = (bf16[512,640]{1,0:T(8,128)(2,1)S(1)}, bf16[512,640]{1,0:T(8,128)(2,1)S(1)}, u32[]{:S(2)}, u32[]{:S(2)}) collective-permute-start(bf16[512,640]{1,0:T(8,128)(2,1)S(1)} %slice.337), channel_id=1, source_target_pairs={{0,32},{4,12},{8,40},{12,20},{16,48},{20,28},{24,56},{28,4},{32,64... | collective-permute-start | bytes 1966088 | tf_op jit(solution)/shard_map/ppermute | solution.py:79
  88.0 28.9 %collective-permute-start.16 = (bf16[512,640]{1,0:T(8,128)(2,1)S(1)}, bf16[512,640]{1,0:T(8,128)(2,1)S(1)}, u32[]{:S(2)}, u32[]{:S(2)}) collective-permute-start(bf16[512,640]{1,0:T(8,128)(2,1)S(1)} %slice.338), channel_id=1, source_target_pairs={{0,96},{4,28},{8,104},{12,4},{16,112},{20,12},{24,120},{28,20},{32... | collective-permute-start | bytes 1966088 | tf_op jit(solution)/shard_map/ppermute | solution.py:79
  109.5 44.1 %collective-permute-start.28 = (bf16[128,960]{1,0:T(8,128)(2,1)}, bf16[128,960]{1,0:T(8,128)(2,1)S(1)}, u32[]{:S(2)}, u32[]{:S(2)}) collective-permute-start(bf16[128,960]{1,0:T(8,128)(2,1)} %slice.344), channel_id=1, source_target_pairs={{0,3},{1,0},{2,1},{3,2},{4,7},{5,4},{6,5},{7,6},{8,11},{9,8},{10,9... | collective-permute-start | bytes 737288 | tf_op jit(solution)/shard_map/ppermute | solution.py:74
  198.4 140.4 %collective-permute-start.47 = (bf16[256,960]{1,0:T(8,128)(2,1)}, bf16[256,960]{1,0:T(8,128)(2,1)}, u32[]{:S(2)}, u32[]{:S(2)}) collective-permute-start(bf16[256,960]{1,0:T(8,128)(2,1)} %get-tuple-element.58), channel_id=1, source_target_pairs={{0,4},{4,0},{8,12},{12,8},{16,20},{20,16},{24,28},{28,24},{32,36},... | collective-permute-start | bytes 1474568 | tf_op jit(solution)/shard_map/ppermute | solution.py:84
  265.1 81.0 %collective-permute-start.68 = (bf16[240,1280]{1,0:T(8,128)(2,1)}, bf16[240,1280]{1,0:T(8,128)(2,1)}, u32[]{:S(2)}, u32[]{:S(2)}) collective-permute-start(bf16[240,1280]{1,0:T(8,128)(2,1)} %get-tuple-element.124), channel_id=1, source_target_pairs={{0,1},{1,2},{2,3},{3,0},{4,5},{5,6},{6,7},{7,4},{8,9},{9,10},{10,1... | collective-permute-start | bytes 1843208 | tf_op jit(solution)/shard_map/ppermute | solution.py:74
  265.5 105.6 %collective-permute-start.69 = (bf16[240,1280]{1,0:T(8,128)(2,1)}, bf16[240,1280]{1,0:T(8,128)(2,1)}, u32[]{:S(2)}, u32[]{:S(2)}) collective-permute-start(bf16[240,1280]{1,0:T(8,128)(2,1)} %get-tuple-element.123), channel_id=1, source_target_pairs={{0,3},{1,0},{2,1},{3,2},{4,7},{5,4},{6,5},{7,6},{8,11},{9,8},{10,9... | collective-permute-start | bytes 1843208 | tf_op jit(solution)/shard_map/ppermute | solution.py:74
  320.7 52.3 %collective-permute-start.70 = (bf16[240,1280]{1,0:T(8,128)(2,1)}, bf16[240,1280]{1,0:T(8,128)(2,1)}, u32[]{:S(2)}, u32[]{:S(2)}) collective-permute-start(bf16[240,1280]{1,0:T(8,128)(2,1)} %get-tuple-element.122), channel_id=1, source_target_pairs={{0,2},{1,3},{2,0},{3,1},{4,6},{5,7},{6,4},{7,5},{8,10},{9,11},{10,... | collective-permute-start | bytes 1843208 | tf_op jit(solution)/shard_map/ppermute | solution.py:74
  338.8 46.6 %collective-permute-start.65 = (bf16[240,960]{1,0:T(8,128)(2,1)}, bf16[240,960]{1,0:T(8,128)(2,1)}, u32[]{:S(2)}, u32[]{:S(2)}) collective-permute-start(bf16[240,960]{1,0:T(8,128)(2,1)} %pad_maximum_fusion.11), channel_id=1, source_target_pairs={{0,3},{1,0},{2,1},{3,2},{4,7},{5,4},{6,5},{7,6},{8,11},{9,8},{10,9... | collective-permute-start | bytes 1382408 | tf_op jit(solution)/shard_map/ppermute | solution.py:74
  340.5 46.3 %collective-permute-start.67 = (bf16[240,960]{1,0:T(8,128)(2,1)}, bf16[240,960]{1,0:T(8,128)(2,1)}, u32[]{:S(2)}, u32[]{:S(2)}) collective-permute-start(bf16[240,960]{1,0:T(8,128)(2,1)} %pad_maximum_fusion.12), channel_id=1, source_target_pairs={{0,1},{1,2},{2,3},{3,0},{4,5},{5,6},{6,7},{7,4},{8,9},{9,10},{10,1... | collective-permute-start | bytes 1382408 | tf_op jit(solution)/shard_map/ppermute | solution.py:74
  372.9 31.0 %collective-permute-start.34 = (bf16[256,960]{1,0:T(8,128)(2,1)}, bf16[256,960]{1,0:T(8,128)(2,1)}, u32[]{:S(2)}, u32[]{:S(2)}) collective-permute-start(bf16[256,960]{1,0:T(8,128)(2,1)} %pad_maximum_fusion.9), channel_id=1, source_target_pairs={{0,3},{1,0},{2,1},{3,2},{4,7},{5,4},{6,5},{7,6},{8,11},{9,8},{10,9... | collective-permute-start | bytes 1474568 | tf_op jit(solution)/shard_map/ppermute | solution.py:74
  378.2 25.8 %collective-permute-start.36 = (bf16[256,960]{1,0:T(8,128)(2,1)}, bf16[256,960]{1,0:T(8,128)(2,1)}, u32[]{:S(2)}, u32[]{:S(2)}) collective-permute-start(bf16[256,960]{1,0:T(8,128)(2,1)} %pad_maximum_fusion.10), channel_id=1, source_target_pairs={{0,1},{1,2},{2,3},{3,0},{4,5},{5,6},{6,7},{7,4},{8,9},{9,10},{10,1... | collective-permute-start | bytes 1474568 | tf_op jit(solution)/shard_map/ppermute | solution.py:74
  414.1 22.0 %collective-permute-start.60 = (bf16[64,832]{0,1:T(8,128)(2,1)S(1)}, bf16[64,832]{0,1:T(8,128)(2,1)S(1)}, u32[]{:S(2)}, u32[]{:S(2)}) collective-permute-start(bf16[64,832]{0,1:T(8,128)(2,1)S(1)} %add_convert_fusion.12), channel_id=1, source_target_pairs={{0,8},{4,36},{8,16},{12,44},{16,24},{20,52},{24,0},{28,60},{32,40}... | collective-permute-start | bytes 319496 | tf_op jit(solution)/shard_map/ppermute | solution.py:79
  414.2 24.5 %collective-permute-start.61 = (bf16[64,832]{0,1:T(8,128)(2,1)S(1)}, bf16[64,832]{0,1:T(8,128)(2,1)S(1)}, u32[]{:S(2)}, u32[]{:S(2)}) collective-permute-start(bf16[64,832]{0,1:T(8,128)(2,1)S(1)} %add_convert_fusion.12), channel_id=1, source_target_pairs={{0,24},{4,100},{8,0},{12,108},{16,8},{20,116},{24,16},{28,124},{32... | collective-permute-start | bytes 319496 | tf_op jit(solution)/shard_map/ppermute | solution.py:79
  416.9 25.0 %collective-permute-start.62 = (bf16[64,832]{0,1:T(8,128)(2,1)S(1)}, bf16[64,832]{0,1:T(8,128)(2,1)S(1)}, u32[]{:S(2)}, u32[]{:S(2)}) collective-permute-start(bf16[64,832]{0,1:T(8,128)(2,1)S(1)} %add_convert_fusion.12), channel_id=1, source_target_pairs={{0,16},{4,68},{8,24},{12,76},{16,0},{20,84},{24,8},{28,92},{32,48}... | collective-permute-start | bytes 319496 | tf_op jit(solution)/shard_map/ppermute | solution.py:79
  417.1 28.6 %collective-permute-start.37 = (bf16[128,960]{1,0:T(8,128)(2,1)S(1)}, bf16[128,960]{1,0:T(8,128)(2,1)}, u32[]{:S(2)}, u32[]{:S(2)}) collective-permute-start(bf16[128,960]{1,0:T(8,128)(2,1)S(1)} %get-tuple-element.170), channel_id=1, source_target_pairs={{0,4},{4,0},{8,12},{12,8},{16,20},{20,16},{24,28},{28,24},{32,36},... | collective-permute-start | bytes 737288 | tf_op jit(solution)/shard_map/ppermute | solution.py:84
  443.6 74.2 %collective-permute-start.63 = (bf16[256,832]{0,1:T(8,128)(2,1)S(1)}, bf16[256,832]{0,1:T(8,128)(2,1)S(1)}, u32[]{:S(2)}, u32[]{:S(2)}) collective-permute-start(bf16[256,832]{0,1:T(8,128)(2,1)S(1)} %dynamic_update_slice.65), channel_id=1, source_target_pairs={{0,4},{4,0},{8,12},{12,8},{16,20},{20,16},{24,28},{28,24},{32,36},... | collective-permute-start | bytes 1277960 | tf_op jit(solution)/shard_map/ppermute | solution.py:84
  (98 other events, 1110.2 us)
Sparse Core Ops, SparseCore 0:
  54.9 44.4 all-gather.1
  389.3 121.0 all-reduce.7
